TPU v7x, 32 devices: a whole 2x2x4 slice. The times are simulated.
32 devices in a mesh: dp: 4 (over y, x), seq: 8 (over z, core).
Axes of the slice: x: 2, y: 2, z: 4, core: 2. Of those that a mesh axis runs over, the one named last changes fastest.
Arguments:
- hidden_in: bfloat16 [8, 4096, 1024], P('dp', 'seq'), may hold values from -6 to 6
- segment_ids: int32 [8, 4096], P('dp'), may hold values from 0 to 256, as said below
- query_weight: bfloat16 [1024, 1024], P(('dp', 'seq')), may hold values from -0.1875 to 0.1875
- query_bias: bfloat16 [1024], P(('dp', 'seq')), may hold values from -3 to 3
- key_weight: bfloat16 [1024, 1024], P(('dp', 'seq')), may hold values from -0.1875 to 0.1875
- value_weight: bfloat16 [1024, 1024], P(('dp', 'seq')), may hold values from -0.1875 to 0.1875
- value_bias: bfloat16 [1024], P(('dp', 'seq')), may hold values from -3 to 3
- output_weight: bfloat16 [1024, 1024], P(('dp', 'seq')), may hold values from -0.5 to 0.5
- output_bias: bfloat16 [1024], P(('dp', 'seq')), may hold values from -3 to 3
- first_gain: bfloat16 [1024], P(('dp', 'seq')), may hold values from 0.5 to 1.5
- first_shift: bfloat16 [1024], P(('dp', 'seq')), may hold values from -3 to 3
- inner_weight: bfloat16 [1024, 4096], P(('dp', 'seq')), may hold values from -0.1875 to 0.1875
- inner_bias: bfloat16 [4096], P(('dp', 'seq')), may hold values from -3 to 3
- outer_weight: bfloat16 [4096, 1024], P(('dp', 'seq')), may hold values from -0.09375 to 0.09375
- outer_bias: bfloat16 [1024], P(('dp', 'seq')), may hold values from -3 to 3
- second_gain: bfloat16 [1024], P(('dp', 'seq')), may hold values from 0.5 to 1.5
- second_shift: bfloat16 [1024], P(('dp', 'seq')), may hold values from -3 to 3
- cotangent: bfloat16 [8, 4096, 1024], P('dp', 'seq'), may hold values from -6 to 6
Outputs:
- layer_out: bfloat16 [8, 4096, 1024], P('dp', 'seq')
- grad_hidden: float32 [8, 4096, 1024], P('dp', 'seq')
- query_weight_grad: float32 [1024, 1024], P(('dp', 'seq'))
- query_bias_grad: float32 [1024], P(('dp', 'seq'))
- key_weight_grad: float32 [1024, 1024], P(('dp', 'seq'))
- value_weight_grad: float32 [1024, 1024], P(('dp', 'seq'))
- value_bias_grad: float32 [1024], P(('dp', 'seq'))
- output_weight_grad: float32 [1024, 1024], P(('dp', 'seq'))
- output_bias_grad: float32 [1024], P(('dp', 'seq'))
- first_gain_grad: float32 [1024], P(('dp', 'seq'))
- first_shift_grad: float32 [1024], P(('dp', 'seq'))
- inner_weight_grad: float32 [1024, 4096], P(('dp', 'seq'))
- inner_bias_grad: float32 [4096], P(('dp', 'seq'))
- outer_weight_grad: float32 [4096, 1024], P(('dp', 'seq'))
- outer_bias_grad: float32 [1024], P(('dp', 'seq'))
- second_gain_grad: float32 [1024], P(('dp', 'seq'))
- second_shift_grad: float32 [1024], P(('dp', 'seq'))
Inputs may be any that keep to these rules, and one draw needn't show every extreme that they name: `segment_ids`: ids never fall along a row and restart for each row; the tokens of a segment are contiguous and its id is positive; 0 marks padding at a row's end, and every row ends in padding. Each segment holds 16 to 256 tokens, a row's first exactly 256, and no segment other than a row's first starts at a position divisible by 512. A row's last segment has the id 4096 // 16.
All inputs are finite; a program needn't handle non-finite values.
Results may differ from a plain program's by a relative error of at most 0.014.
Values may be sent and summed in bfloat16 or wider, within the bound.
A program may use at most 256 MiB of HBM per device.

v0:
```python
import functools

import jax
import jax.numpy as jnp
from jax import lax
from jax.experimental import pallas as pl
from jax.experimental.pallas import tpu as pltpu
from jax.sharding import PartitionSpec as P

HD = 64
SEGMAX = 256
EPS = 1e-05
LOG2E = 1.4426950408889634
SCORE_SCALE = 0.125 * LOG2E
HIDDEN = -1e30
PAIR = 2 * HD
MESH = pl.DeviceIdType.MESH
BF16 = jnp.bfloat16
F32 = jnp.float32
VMEM = 64 * 2**20


group_heads = 4


def passed_along(block, axis, distance):
    devices = range(lax.axis_size(axis))
    route = [(i - distance, i) for i in devices if i - distance in devices]
    return lax.ppermute(block, axis, route)


def normalize(hidden, gain, shift):
    center = hidden - jnp.mean(hidden, axis=-1, keepdims=True)
    spread = jnp.mean(center * center, axis=-1, keepdims=True)
    return center * lax.rsqrt(spread + 1e-05) * gain + shift


def contract_rows(left, right):
    return lax.dot_general(
        left, right, (((0,), (0,)), ((), ())), preferred_element_type=jnp.float32
    )


def times_transposed(left, right):
    return lax.dot_general(
        left, right, (((1,), (1,)), ((), ())), preferred_element_type=jnp.float32
    )


def column_sum(values):
    return jnp.sum(values.astype(jnp.float32), axis=0)


def plain(
    hidden_in,
    segment_ids,
    query_weight,
    query_bias,
    key_weight,
    value_weight,
    value_bias,
    output_weight,
    output_bias,
    first_gain,
    first_shift,
    inner_weight,
    inner_bias,
    outer_weight,
    outer_bias,
    second_gain,
    second_shift,
    cotangent,
):
    rows_here, tokens, width = hidden_in.shape
    window = tokens + SEGMAX
    span = group_heads * HD
    groups = width // span
    items = jnp.arange(rows_here * groups, dtype=jnp.int32)
    (
        query_matrix,
        query_offset,
        key_matrix,
        value_matrix,
        value_offset,
        output_matrix,
        output_offset,
        first_scale,
        first_offset,
    ) = (
        lax.all_gather(query_weight, ("dp", "seq"), axis=0, tiled=True),
        lax.all_gather(query_bias, ("dp", "seq"), axis=0, tiled=True),
        lax.all_gather(key_weight, ("dp", "seq"), axis=0, tiled=True),
        lax.all_gather(value_weight, ("dp", "seq"), axis=0, tiled=True),
        lax.all_gather(value_bias, ("dp", "seq"), axis=0, tiled=True),
        lax.all_gather(output_weight, ("dp", "seq"), axis=0, tiled=True),
        lax.all_gather(output_bias, ("dp", "seq"), axis=0, tiled=True),
        lax.all_gather(first_gain, ("dp", "seq"), axis=0, tiled=True),
        lax.all_gather(first_shift, ("dp", "seq"), axis=0, tiled=True),
    )
    flat = hidden_in.reshape(rows_here * tokens, width)
    offset = lax.axis_index("seq") * tokens
    padded_ids = jnp.concatenate(
        [jnp.full((rows_here, SEGMAX), -1, jnp.int32), segment_ids], axis=1
    )
    key_ids = lax.dynamic_slice_in_dim(padded_ids, offset, window, 1)
    query_ids = key_ids[:, SEGMAX:]
    diagonal = jnp.arange(window)[None, :] == jnp.arange(tokens)[:, None] + SEGMAX
    visible = (query_ids[:, :, None] == key_ids[:, None, :]) & (
        query_ids[:, :, None] > 0
    ) | diagonal[None]
    queries = (
        (
            jnp.dot(flat, query_matrix, preferred_element_type=jnp.float32)
            + query_offset.astype(jnp.float32)
        )
        .astype(jnp.bfloat16)
        .reshape(rows_here, tokens, width)
    )
    keys_own = (
        jnp.dot(flat, key_matrix, preferred_element_type=jnp.float32)
        .astype(jnp.bfloat16)
        .reshape(rows_here, tokens, width)
    )
    values_own = (
        (
            jnp.dot(flat, value_matrix, preferred_element_type=jnp.float32)
            + value_offset.astype(jnp.float32)
        )
        .astype(jnp.bfloat16)
        .reshape(rows_here, tokens, width)
    )
    tails = passed_along(
        (keys_own[:, tokens - SEGMAX :], values_own[:, tokens - SEGMAX :]), "seq", 1
    )
    keys_all = jnp.concatenate([tails[0], keys_own], axis=1)
    values_all = jnp.concatenate([tails[1], values_own], axis=1)

    def pieces(item):
        row = item // groups
        column = item % groups * span
        query_part = lax.dynamic_slice(queries, (row, 0, column), (1, tokens, span))[0].reshape(
            tokens, group_heads, HD
        )
        key_part = lax.dynamic_slice(keys_all, (row, 0, column), (1, window, span))[0].reshape(
            window, group_heads, HD
        )
        value_part = lax.dynamic_slice(values_all, (row, 0, column), (1, window, span))[0].reshape(
            window, group_heads, HD
        )
        mask_row = lax.dynamic_index_in_dim(visible, row, 0, keepdims=False)
        scores = (
            jnp.einsum("qhd,khd->hqk", query_part, key_part, preferred_element_type=jnp.float32)
            * 0.125
        )
        scores = jnp.where(mask_row[None], scores, -1e30)
        return (row, column, query_part, key_part, value_part, scores)

    def attend(item):
        row, column, query_part, key_part, value_part, scores = pieces(item)
        highest = jnp.max(scores, axis=-1, keepdims=True)
        expo = jnp.exp(scores - highest)
        total = jnp.sum(expo, axis=-1, keepdims=True)
        probs = (expo / total).astype(jnp.bfloat16)
        mixed_part = jnp.einsum(
            "hqk,khd->qhd", probs, value_part, preferred_element_type=jnp.float32
        )
        return (
            mixed_part.astype(jnp.bfloat16).reshape(tokens, span),
            highest[..., 0] + jnp.log(total[..., 0]),
        )

    mixed_parts, logsums = lax.map(attend, items)
    mixed = (
        mixed_parts.reshape(rows_here, groups, tokens, span)
        .transpose(0, 2, 1, 3)
        .reshape(rows_here * tokens, width)
    )
    first_sum = (
        flat.astype(jnp.float32)
        + jnp.dot(mixed, output_matrix, preferred_element_type=jnp.float32)
        + output_offset.astype(jnp.float32)
    )
    normed = normalize(first_sum, first_scale.astype(jnp.float32), first_offset.astype(jnp.float32))
    normed_low = normed.astype(jnp.bfloat16)
    inner_matrix, inner_offset, outer_matrix, outer_offset, second_scale, second_offset = (
        lax.all_gather(inner_weight, ("dp", "seq"), axis=0, tiled=True),
        lax.all_gather(inner_bias, ("dp", "seq"), axis=0, tiled=True),
        lax.all_gather(outer_weight, ("dp", "seq"), axis=0, tiled=True),
        lax.all_gather(outer_bias, ("dp", "seq"), axis=0, tiled=True),
        lax.all_gather(second_gain, ("dp", "seq"), axis=0, tiled=True),
        lax.all_gather(second_shift, ("dp", "seq"), axis=0, tiled=True),
    )
    inner = jnp.dot(
        normed_low, inner_matrix, preferred_element_type=jnp.float32
    ) + inner_offset.astype(jnp.float32)
    active_low = jax.nn.gelu(inner, approximate=False).astype(jnp.bfloat16)
    second_sum = (
        normed
        + jnp.dot(active_low, outer_matrix, preferred_element_type=jnp.float32)
        + outer_offset.astype(jnp.float32)
    )
    layer_out = normalize(
        second_sum, second_scale.astype(jnp.float32), second_offset.astype(jnp.float32)
    )
    layer_out = layer_out.astype(jnp.bfloat16).reshape(rows_here, tokens, width)
    inner_matrix, inner_offset, outer_matrix, outer_offset, second_scale, second_offset = (
        lax.all_gather(inner_weight, ("dp", "seq"), axis=0, tiled=True),
        lax.all_gather(inner_bias, ("dp", "seq"), axis=0, tiled=True),
        lax.all_gather(outer_weight, ("dp", "seq"), axis=0, tiled=True),
        lax.all_gather(outer_bias, ("dp", "seq"), axis=0, tiled=True),
        lax.all_gather(second_gain, ("dp", "seq"), axis=0, tiled=True),
        lax.all_gather(second_shift, ("dp", "seq"), axis=0, tiled=True),
    )
    upstream = cotangent.reshape(rows_here * tokens, width).astype(jnp.float32)
    _, pull_second = jax.vjp(
        normalize, second_sum, second_scale.astype(jnp.float32), second_offset.astype(jnp.float32)
    )
    grad_second, second_gain_grad, second_shift_grad = pull_second(upstream)
    outer_grad = grad_second.astype(jnp.bfloat16)
    outer_weight_grad = contract_rows(active_low, outer_grad)
    outer_bias_grad = column_sum(outer_grad)
    _, pull_gelu = jax.vjp(lambda value: jax.nn.gelu(value, approximate=False), inner)
    (inner_grad_full,) = pull_gelu(times_transposed(outer_grad, outer_matrix))
    inner_grad = inner_grad_full.astype(jnp.bfloat16)
    inner_weight_grad = contract_rows(normed_low, inner_grad)
    inner_bias_grad = column_sum(inner_grad)
    grad_normed = grad_second + times_transposed(inner_grad, inner_matrix)
    (
        query_matrix,
        query_offset,
        key_matrix,
        value_matrix,
        value_offset,
        output_matrix,
        output_offset,
        first_scale,
        first_offset,
    ) = (
        lax.all_gather(query_weight, ("dp", "seq"), axis=0, tiled=True),
        lax.all_gather(query_bias, ("dp", "seq"), axis=0, tiled=True),
        lax.all_gather(key_weight, ("dp", "seq"), axis=0, tiled=True),
        lax.all_gather(value_weight, ("dp", "seq"), axis=0, tiled=True),
        lax.all_gather(value_bias, ("dp", "seq"), axis=0, tiled=True),
        lax.all_gather(output_weight, ("dp", "seq"), axis=0, tiled=True),
        lax.all_gather(output_bias, ("dp", "seq"), axis=0, tiled=True),
        lax.all_gather(first_gain, ("dp", "seq"), axis=0, tiled=True),
        lax.all_gather(first_shift, ("dp", "seq"), axis=0, tiled=True),
    )
    _, pull_first = jax.vjp(
        normalize, first_sum, first_scale.astype(jnp.float32), first_offset.astype(jnp.float32)
    )
    grad_first, first_gain_grad, first_shift_grad = pull_first(grad_normed)
    attn_grad = grad_first.astype(jnp.bfloat16)
    output_weight_grad = contract_rows(mixed, attn_grad)
    output_bias_grad = column_sum(attn_grad)
    grad_mixed = (
        times_transposed(attn_grad, output_matrix)
        .astype(jnp.bfloat16)
        .reshape(rows_here, tokens, width)
    )

    def attend_back(item):
        row, column, query_part, key_part, value_part, scores = pieces(item)
        logsum = lax.dynamic_index_in_dim(logsums, item, 0, keepdims=False)
        grad_part = lax.dynamic_slice(grad_mixed, (row, 0, column), (1, tokens, span))[0].reshape(
            tokens, group_heads, HD
        )
        probs = jnp.exp(scores - logsum[..., None])
        dprob = jnp.einsum(
            "qhd,khd->hqk", grad_part, value_part, preferred_element_type=jnp.float32
        )
        delta = jnp.sum(probs * dprob, axis=-1, keepdims=True)
        score_grad = (probs * (dprob - delta)).astype(jnp.bfloat16)
        query_part_grad = (
            jnp.einsum("hqk,khd->qhd", score_grad, key_part, preferred_element_type=jnp.float32)
            * 0.125
        )
        key_part_grad = (
            jnp.einsum("hqk,qhd->khd", score_grad, query_part, preferred_element_type=jnp.float32)
            * 0.125
        )
        value_part_grad = jnp.einsum(
            "hqk,qhd->khd",
            probs.astype(jnp.bfloat16),
            grad_part,
            preferred_element_type=jnp.float32,
        )
        return (
            query_part_grad.reshape(tokens, span),
            key_part_grad.reshape(window, span),
            value_part_grad.reshape(window, span),
        )

    query_parts, key_parts, value_parts = lax.map(attend_back, items)
    query_full = (
        query_parts.reshape(rows_here, groups, tokens, span)
        .transpose(0, 2, 1, 3)
        .reshape(rows_here * tokens, width)
    )
    key_window = (
        key_parts.reshape(rows_here, groups, window, span)
        .transpose(0, 2, 1, 3)
        .reshape(rows_here, window, width)
    )
    value_window = (
        value_parts.reshape(rows_here, groups, window, span)
        .transpose(0, 2, 1, 3)
        .reshape(rows_here, window, width)
    )
    returned = (
        passed_along(key_window[:, :SEGMAX].astype(jnp.bfloat16), "seq", -1).astype(jnp.float32),
        passed_along(value_window[:, :SEGMAX].astype(jnp.bfloat16), "seq", -1).astype(jnp.float32),
    )
    key_own = key_window[:, SEGMAX:]
    value_own = value_window[:, SEGMAX:]
    key_total = jnp.concatenate(
        [key_own[:, : tokens - SEGMAX], key_own[:, tokens - SEGMAX :] + returned[0]], axis=1
    )
    value_total = jnp.concatenate(
        [value_own[:, : tokens - SEGMAX], value_own[:, tokens - SEGMAX :] + returned[1]], axis=1
    )
    query_grad = query_full.astype(jnp.bfloat16)
    key_grad = key_total.reshape(rows_here * tokens, width).astype(jnp.bfloat16)
    value_grad = value_total.reshape(rows_here * tokens, width).astype(jnp.bfloat16)
    query_weight_grad = contract_rows(flat, query_grad)
    query_bias_grad = column_sum(query_grad)
    key_weight_grad = contract_rows(flat, key_grad)
    value_weight_grad = contract_rows(flat, value_grad)
    value_bias_grad = column_sum(value_grad)
    grad_hidden = (
        grad_first
        + times_transposed(query_grad, query_matrix)
        + times_transposed(key_grad, key_matrix)
        + times_transposed(value_grad, value_matrix)
    ).reshape(rows_here, tokens, width)
    shards = (
        lax.psum_scatter(query_weight_grad, ("dp", "seq"), scatter_dimension=0, tiled=True),
        lax.psum_scatter(query_bias_grad, ("dp", "seq"), scatter_dimension=0, tiled=True),
        lax.psum_scatter(key_weight_grad, ("dp", "seq"), scatter_dimension=0, tiled=True),
        lax.psum_scatter(value_weight_grad, ("dp", "seq"), scatter_dimension=0, tiled=True),
        lax.psum_scatter(value_bias_grad, ("dp", "seq"), scatter_dimension=0, tiled=True),
        lax.psum_scatter(output_weight_grad, ("dp", "seq"), scatter_dimension=0, tiled=True),
        lax.psum_scatter(output_bias_grad, ("dp", "seq"), scatter_dimension=0, tiled=True),
        lax.psum_scatter(first_gain_grad, ("dp", "seq"), scatter_dimension=0, tiled=True),
        lax.psum_scatter(first_shift_grad, ("dp", "seq"), scatter_dimension=0, tiled=True),
        lax.psum_scatter(inner_weight_grad, ("dp", "seq"), scatter_dimension=0, tiled=True),
        lax.psum_scatter(inner_bias_grad, ("dp", "seq"), scatter_dimension=0, tiled=True),
        lax.psum_scatter(outer_weight_grad, ("dp", "seq"), scatter_dimension=0, tiled=True),
        lax.psum_scatter(outer_bias_grad, ("dp", "seq"), scatter_dimension=0, tiled=True),
        lax.psum_scatter(second_gain_grad, ("dp", "seq"), scatter_dimension=0, tiled=True),
        lax.psum_scatter(second_shift_grad, ("dp", "seq"), scatter_dimension=0, tiled=True),
    )
    return (
        layer_out,
        grad_hidden,
        shards[0],
        shards[1],
        shards[2],
        shards[3],
        shards[4],
        shards[5],
        shards[6],
        shards[7],
        shards[8],
        shards[9],
        shards[10],
        shards[11],
        shards[12],
        shards[13],
        shards[14],
    )


GRID = (2, 2, 4, 2)
FF_PARTS = 8
PART = 512
EARLY = 5
PIECE = GRID + (32, PART)


class Place:
    def __init__(self):
        dp = lax.axis_index("dp")
        seq = lax.axis_index("seq")
        self.x = lax.rem(dp, 2)
        self.y = lax.div(dp, 2)
        self.z = lax.div(seq, 2)
        self.c = lax.rem(seq, 2)
        self.seq = seq

    def device(self, x=None, y=None, z=None, c=None):
        x = self.x if x is None else x
        y = self.y if y is None else y
        z = self.z if z is None else z
        c = self.c if c is None else c
        return (y * 2 + x, z * 2 + c)

    def peer(self, dim):
        if dim == "x":
            return self.device(x=1 - self.x)
        if dim == "y":
            return self.device(y=1 - self.y)
        if dim == "c":
            return self.device(c=1 - self.c)
        return self.device(z=lax.rem(self.z + dim, 4))


def signal(semaphore, device):
    pl.semaphore_signal(semaphore, inc=1, device_id=device, device_id_type=MESH)


def meet(place, along=0):
    barrier = pltpu.get_barrier_semaphore()
    for dim in ("x", "y", "c", 1, 2, 3):
        signal(barrier, place.peer(dim))
    extra = 0
    if along:
        up = (place.c == 1) & (place.z < 3)
        down = (place.c == 0) & (place.z > 0)
        receives, sends = (down, up) if along > 0 else (up, down)
        other = lax.rem(place.z + (3 if along > 0 else 1), 4)

        @pl.when(receives)
        def _():
            signal(barrier, place.device(z=other, c=1 - place.c))

        extra = sends.astype(jnp.int32)
    pl.semaphore_wait(barrier, 6 + extra)


def remote(src, dst, send, recv, device):
    return pltpu.make_async_remote_copy(
        src_ref=src, dst_ref=dst, send_sem=send, recv_sem=recv, device_id=device, device_id_type=MESH
    )


class Gather:
    def __init__(self, place, order, source, target, send, recv):
        held = {"x": False, "y": False, "z": False}

        def region():
            index = []
            for name, size in (("y", 2), ("x", 2), ("z", 4)):
                index.append(pl.ds(0, size) if held[name] else pl.ds(getattr(place, name), 1))
            return target(index[0], index[1], index[2], pl.ds(place.c, 1))

        self.own = pltpu.make_async_copy(source, region(), recv.at[6])
        self.phases = []
        for number, dim in enumerate(order):
            here = region()
            copies = []
            for partner in (1, 2, 3) if dim == "z" else (dim,):
                slot = partner - 1 if dim == "z" else {"x": 3, "y": 4}[dim]
                copies.append(
                    remote(
                        source if number == 0 else here,
                        here,
                        send.at[slot],
                        recv.at[slot],
                        place.peer(partner),
                    )
                )
            self.phases.append(copies)
            held[dim] = True
        here = region()
        self.phases.append([remote(here, here, send.at[5], recv.at[5], place.peer("c"))])

    def start(self, phase):
        if phase == 0:
            self.own.start()
        for copy in self.phases[phase]:
            copy.start()

    def arrive(self, phase):
        for copy in self.phases[phase]:
            copy.wait_recv()
        if phase == 0:
            self.own.wait()

    def step(self, phase):
        if phase > 0:
            self.arrive(phase - 1)
        if phase < 4:
            self.start(phase)

    def finish(self):
        for copies in self.phases:
            for copy in copies:
                copy.wait_send()


class Sums:
    def __init__(self, place, count, stage, slot, bufs, store, halves=2, ready=None, order=None, offsets=(0, 1, 3, 5, 7)):
        self.place, self.count, self.stage, self.slot = place, count, stage, slot
        self.order, self.offsets = order, offsets
        self.r0, self.r1, self.r2, self.r3, self.send, self.recv = bufs
        self.store, self.halves, self.ready = store, halves, ready

    def copies(self, j, half, phase):
        place = self.place
        send, recv = self.send.at[j, half], self.recv.at[j, half]
        r0, r1, r2, r3 = (ref.at[j, half] for ref in (self.r0, self.r1, self.r2, self.r3))
        if phase == 0:
            source = self.stage.at[self.slot(j), :, :, :, 1 - place.c, pl.ds(16 * half, 16)]
            return [remote(source, r0, send.at[0], recv.at[0], place.peer("c"))]
        if phase == 1:
            source, dim = (r0.at[1 - place.y], "y") if half == 0 else (r0.at[:, 1 - place.x], "x")
            return [remote(source, r1, send.at[1], recv.at[1], place.peer(dim))]
        if phase == 2:
            source, dim = (r1.at[1 - place.x], "x") if half == 0 else (r1.at[1 - place.y], "y")
            return [remote(source, r2, send.at[2], recv.at[2], place.peer(dim))]
        return [
            remote(r2.at[lax.rem(place.z + k, 4)], r3.at[k - 1], send.at[2 + k], recv.at[2 + k], place.peer(k))
            for k in (1, 2, 3)
        ]

    def step(self, j, phase):
        place = self.place
        if phase == 0 and self.ready is not None:
            self.ready(j)
        for half in range(self.halves):
            if phase > 0:
                for copy in self.copies(j, half, phase - 1):
                    copy.wait_recv()
            if phase == 1:
                self.copies(j, half, 0)[0].wait_send()
                mine = self.stage[self.slot(j), :, :, :, place.c, 16 * half : 16 * half + 16, :]
                self.r0[j, half] = self.r0[j, half] + mine
            elif phase == 2:
                mine = self.r0[j, half, place.y] if half == 0 else self.r0[j, half, :, place.x]
                self.r1[j, half] = self.r1[j, half] + mine
            elif phase == 3:
                mine = self.r1[j, half, place.x] if half == 0 else self.r1[j, half, place.y]
                self.r2[j, half] = self.r2[j, half] + mine
            elif phase == 4:
                total = self.r2[j, half, place.z].astype(F32)
                for k in range(3):
                    total = total + self.r3[j, half, k].astype(F32)
                self.store(j, half, total)
            if phase < 4:
                for copy in self.copies(j, half, phase):
                    copy.start()

    def tick(self, time):
        for phase, offset in enumerate(self.offsets):
            j = time - offset
            valid = (j >= 0) & (j < self.count)
            if self.order is not None:
                j, valid = self.order(j)
            if isinstance(valid, bool):
                if valid:
                    self.step(j, phase)
            else:
                pl.when(valid)(functools.partial(self.step, j, phase))

    def finish(self):
        def body(j, carry):
            for half in range(self.halves):
                for phase in (1, 2, 3):
                    for copy in self.copies(j, half, phase):
                        copy.wait_send()
            return carry

        lax.fori_loop(0, self.count, body, 0)


def sums_buffers(count, columns=512, halves=2):
    block = (16, columns)
    return [
        pltpu.VMEM((count, halves, 2, 2, 4) + block, BF16),
        pltpu.VMEM((count, halves, 2, 4) + block, BF16),
        pltpu.VMEM((count, halves, 4) + block, BF16),
        pltpu.VMEM((count, halves, 3) + block, BF16),
        pltpu.SemaphoreType.DMA((count, halves, 6)),
        pltpu.SemaphoreType.DMA((count, halves, 6)),
    ]


def advance(slots, time, offsets):
    for phase, offset in enumerate(offsets):
        number = time - offset
        if 0 <= number < len(slots):
            for part in slots[number]:
                part.step(phase)


def dot(left, right):
    return jnp.dot(left, right, preferred_element_type=F32)


def dot_nt(left, right):
    return lax.dot_general(left, right, (((1,), (1,)), ((), ())), preferred_element_type=F32)


def dot_tn(left, right):
    return lax.dot_general(left, right, (((0,), (0,)), ((), ())), preferred_element_type=F32)


def spread(blocks, row, base, shift, count):
    at = lax.broadcasted_iota(jnp.int32, (32, 16, 128), 1)
    rows = jnp.sum(jnp.where(at == row, blocks.reshape(32, 16, 128).astype(F32), 0.0), axis=1)
    lane = lax.broadcasted_iota(jnp.int32, (128, count), 0)
    column = lax.broadcasted_iota(jnp.int32, (128, count), 1)
    pick = jnp.where(lane == base + (column & (2**shift - 1)), 1.0, 0.0).astype(BF16)
    wide = dot(rows.astype(BF16), pick)
    device = lax.broadcasted_iota(jnp.int32, (32, count), 0)
    column = lax.broadcasted_iota(jnp.int32, (32, count), 1)
    return jnp.sum(jnp.where(device == column >> shift, wide, 0.0), axis=0, keepdims=True)


BEATS = (0, 1, 2, 3, 4)
ITEM_BEATS = {0: 11, 3: 12, 7: 13, 10: 14, 14: 15}
PART_BEATS = {1: 16, 4: 17, 7: 18}
EVEN = (("zxy", 4), ("zyx", 4))
MIXED = (("zxy", 3), ("zyx", 3), ("xzy", 1), ("yzx", 1))


def gather_slots(place, source, target, pieces, orders, send, recv):
    slots = []
    number = 0
    for rows, first, columns in pieces:
        slot = []
        for order, eighths in orders:
            cols = pl.ds(first, columns * eighths // 8)
            first += columns * eighths // 8
            slot.append(
                Gather(
                    place,
                    order,
                    source.at[:, :, :, :, rows, cols],
                    lambda y, x, z, c, rows=rows, cols=cols: target.at[y, x, z, c, rows, cols],
                    send.at[number],
                    recv.at[number],
                )
            )
            number += 1
        slots.append(slot)
    return slots


def finish_slots(slots):
    for slot in slots:
        for part in slot:
            part.finish()


def mask_scores(key_ids, query_ids):
    keys, queries = key_ids.shape[0], query_ids.shape[1]
    key_at = lax.broadcasted_iota(jnp.int32, (keys, queries), 0)
    query_at = lax.broadcasted_iota(jnp.int32, (keys, queries), 1)
    visible = ((key_ids == query_ids) & (query_ids > 0)) | (key_at == query_at + SEGMAX)
    return jnp.where(visible, 0.0, HIDDEN).astype(F32)


BLOCK = 128


def key_ranges(tokens):
    window = tokens + SEGMAX
    return [(start, min(start + BLOCK + 2 * SEGMAX, window)) for start in range(0, tokens, BLOCK)]


def one_head(block, head):
    lane = lax.broadcasted_iota(jnp.int32, block.shape, 1)
    return jnp.where((lane >= HD) == bool(head), block, jnp.zeros_like(block))


def both_heads(block):
    return jnp.concatenate([one_head(block, 0), one_head(block, 1)], axis=0)


def own_heads(value):
    return jnp.concatenate([value[:HD, :BLOCK], value[HD:, BLOCK:]], axis=0)


def layer_norm(value):
    center = value - jnp.mean(value, axis=-1, keepdims=True)
    scale = lax.rsqrt(jnp.mean(center * center, axis=-1, keepdims=True) + EPS)
    return center * scale, scale


def layer_norm_back(grad, unit, scale):
    return scale * (
        grad
        - jnp.mean(grad, axis=-1, keepdims=True)
        - unit * jnp.mean(grad * unit, axis=-1, keepdims=True)
    )


def gelu_both(value):
    bell = jnp.exp2(value * value * (-0.5 * LOG2E)) * 0.3989422804014327
    below = 0.5 + 0.5 * lax.erf(value * 0.7071067811865476)
    return value * below, below + value * bell


def encode_kernel(
    x_in, key_ids, query_ids, v0, v1, v2, v3, v4, v5, v6, v7, v8, wq_in, wk_in, wv_in, wo_in, inner_in, outer_in,
    q_out, k_out, v_out, xt_out, w_out, mixed_out, unit_out, low_out, inner_out, outer_out, active_out, slope_out,
    lse, scale, vec,
    weights, small, smalls, xt, q, k, v, mixed, unit, low, bias, inner, own_weights, inner_own, outer_own, inner_b, active, slope,
    send, recv, tail_sem, local_sem, part_sem, weight_sem,
):
    place = Place()
    tokens, width = x_in.shape[1], x_in.shape[2]
    own_x = pltpu.make_async_copy(x_in, xt.at[:, pl.ds(SEGMAX, tokens)], local_sem.at[0])
    own_x.start()
    own_ff = [
        pltpu.make_async_copy(inner_in, inner_own, local_sem.at[22]),
        pltpu.make_async_copy(outer_in, outer_own, local_sem.at[23]),
    ]
    own_w = [
        pltpu.make_async_copy(source, own_weights.at[number], local_sem.at[18 + number])
        for number, source in enumerate((wq_in, wk_in, wv_in, wo_in))
    ]
    for copy in own_w + own_ff:
        copy.start()
    at = lax.broadcasted_iota(jnp.int32, (16, 128), 0)
    block = jnp.zeros((16, 128), F32)
    for number, vector in enumerate((v0, v1, v2, v3, v4, v5, v6, v7, v8)):
        size = vector.shape[1]
        base, row = (number % 4 * 32, number // 4) if number < 8 else (0, 2)
        lane = lax.broadcasted_iota(jnp.int32, (size, 128), 1)
        index = lax.broadcasted_iota(jnp.int32, (size, 128), 0)
        pick = jnp.where(lane == base + index, 1.0, 0.0).astype(BF16)
        wide = dot(jnp.broadcast_to(vector[...], (16, size)), pick)
        block = block + jnp.where(at == row, wide, 0.0)
    small[0, 0, 0, 0] = block.astype(BF16)
    meet(place, 1)
    half = width // 2
    slots = []
    vectors = Gather(place, "zxy", small, lambda y, x, z, c: smalls.at[y, x, z, c], send.at[56], recv.at[56])
    everything, used = slice(None), 0

    def add(source, target, pieces, orders):
        nonlocal used, slots
        sems = pl.ds(used, len(orders) * len(pieces))
        used += len(orders) * len(pieces)
        slots += gather_slots(place, source, target, pieces, orders, send.at[sems], recv.at[sems])

    for copy in own_w:
        copy.wait()
    for matrix in range(3):
        add(own_weights.at[matrix], w_out.at[matrix], [(everything, part * half, half) for part in range(2)], EVEN)
    add(own_weights.at[3], w_out.at[3], [(everything, 0, width)], MIXED)
    slots[0].append(vectors)
    add(inner_own, inner_out, [(everything, part * width, width) for part in range(4)], MIXED)
    add(outer_own, outer_out, [(pl.ds(part * 32, 32), 0, width) for part in range(4)], MIXED)

    tails = []
    for row in range(2):
        for start in range(0, SEGMAX, 128):
            tails.append(
                remote(
                    x_in.at[row, pl.ds(tokens - SEGMAX + start, 128)],
                    xt.at[row, pl.ds(start, 128)],
                    tail_sem.at[0, len(tails)],
                    tail_sem.at[1, len(tails)],
                    place.device(z=lax.rem(place.z + place.c, 4), c=1 - place.c),
                )
            )
    has_next, has_last = place.seq < 7, place.seq > 0
    saves = []

    def save(source, target):
        copy = pltpu.make_async_copy(source, target, local_sem.at[1 + len(saves)])
        copy.start()
        saves.append(copy)

    def project(matrix, part):
        target, bias_row, first = ((q, 0, SEGMAX), (k, None, 0), (v, 1, 0))[matrix]
        columns = slice(part * half, part * half + half)
        right = weights[matrix, :, :, :, :, :, columns].reshape(width, half)
        for row in range(2):
            out = dot(xt[row, first:, :], right)
            if bias_row is not None:
                out = out + vec[bias_row : bias_row + 1, columns]
            target[row, :, columns] = out.astype(BF16)

    weight_loads = []
    for matrix in range(4):
        for start in range(0, width, half):
            columns = pl.ds(start, half) if matrix < 3 else pl.ds(0, width)
            if matrix < 3 or start == 0:
                weight_loads.append(
                    pltpu.make_async_copy(
                        w_out.at[matrix, :, :, :, :, :, columns],
                        weights.at[matrix, :, :, :, :, :, columns],
                        weight_sem.at[len(weight_loads)],
                    )
                )
    last = BEATS[-1]
    for time in range(last + 7):
        if 3 <= time <= 6:
            pl.when(has_next)(tails[time - 3].start)
        if time == 3:
            xt_zero = jnp.zeros((2, SEGMAX, width), BF16)

            @pl.when(place.seq == 0)
            def _():
                xt[:, :SEGMAX, :] = xt_zero

            own_x.wait()
            for copy in own_ff:
                copy.wait()
        advance(slots, time, BEATS)
        done = time - last
        if done == 0:
            for vector in range(8):
                vec[vector : vector + 1, :] = spread(smalls[...], vector // 4, vector % 4 * 32, 5, width)
            vec[8:, :] = jnp.zeros((8, width), F32)
            for part in range(FF_PARTS):
                for device in range(4):
                    index = part * 4 + device
                    row = smalls[index // 16, index // 8 % 2, index // 2 % 4, index % 2]
                    inner_b[part, :, device * 128 : device * 128 + 128] = row[2:3, :].astype(F32)
        if done >= 0:
            weight_loads[done].start()
        if done >= 1:
            matrix, part = (done - 1) // 2, (done - 1) % 2
            weight_loads[done - 1].wait()
            if matrix == 1 and part == 0:
                for tail in tails:
                    pl.when(has_last)(tail.wait_recv)
                save(xt, xt_out)
            project(matrix, part)
            if part == 1:
                save((q, k, v)[matrix], (q_out, k_out, v_out)[matrix])

    pairs = width // PAIR
    count = 2 * pairs
    item_beats = ITEM_BEATS
    part_beats = PART_BEATS

    def beat(time):
        advance(slots, time, BEATS)

    def inner_load(part):
        columns = pl.ds(part * PART if isinstance(part, int) else pl.multiple_of(part * PART, PART), PART)
        ring = part % 2
        return pltpu.make_async_copy(inner_out.at[:, :, :, :, :, columns], inner.at[ring], weight_sem.at[7 + ring])

    def attend(item, carry):
        row, pair = lax.div(item, pairs), lax.rem(item, pairs)
        for number, time in item_beats.items():
            pl.when(item == number)(functools.partial(beat, time))

        @pl.when(pair == 0)
        def _():
            bias[...] = mask_scores(key_ids[row], query_ids[row])

        columns = pl.ds(pl.multiple_of(pair * PAIR, PAIR), PAIR)
        v_t = v[row, :, columns].T
        for start, (low_key, high_key) in zip(range(0, tokens, BLOCK), key_ranges(tokens)):
            s = dot_nt(k[row, low_key:high_key, columns], both_heads(q[row, start : start + BLOCK, columns]))
            mask = bias[low_key:high_key, start : start + BLOCK]
            s = s * SCORE_SCALE + jnp.concatenate([mask, mask], axis=1)
            highest = jnp.max(s, axis=0, keepdims=True)
            expo = jnp.exp2(s - highest)
            total = jnp.sum(expo, axis=0, keepdims=True)
            out = dot(v_t[:, low_key:high_key], expo.astype(BF16)) * (1.0 / total)
            logs = highest + jnp.log2(total)
            for head in range(2):
                lse[row, pair, head : head + 1, start : start + BLOCK] = logs[:, head * BLOCK : head * BLOCK + BLOCK]
            mixed[row, start : start + BLOCK, columns] = own_heads(out).T.astype(BF16)

        @pl.when(pair == pairs - 1)
        def _():
            pl.when(row == 0)(weight_loads[6].wait)
            matrix = weights[3].reshape(width, width)
            for start in range(0, tokens, 256):
                rows = pl.ds(start, 256)
                residual = xt[row, SEGMAX + start : SEGMAX + start + 256, :].astype(F32)
                total = dot(mixed[row, rows, :], matrix) + residual + vec[2:3, :]
                centered, spread_ = layer_norm(total)
                unit[row, rows, :] = centered
                scale[row, rows, :] = spread_
                low[row, rows, :] = (centered * vec[3:4, :] + vec[4:5, :]).astype(BF16)

        return carry

    lax.fori_loop(0, count, attend, 0)
    for source, target in ((mixed, mixed_out), (unit, unit_out), (low, low_out)):
        save(source, target)

    def part_saves(part):
        columns = pl.ds(part * PART if isinstance(part, int) else pl.multiple_of(part * PART, PART), PART)
        ring = part % 2
        return [
            pltpu.make_async_copy(source.at[ring], target.at[:, columns], part_sem.at[number, ring])
            for number, (source, target) in enumerate(((active, active_out), (slope, slope_out)))
        ]

    def feed(part, carry):
        for number, time in part_beats.items():
            pl.when(part == number)(functools.partial(beat, time))

        @pl.when(part >= 2)
        def _():
            for copy in part_saves(part - 2):
                copy.wait()

        ring = lax.rem(part, 2)
        inner_load(part).wait()
        pl.when(part + 1 < FF_PARTS)(lambda: inner_load(part + 1).start())
        w1 = inner[ring].reshape(width, PART)
        for row in range(2):
            act, der = gelu_both(dot(low[row], w1) + inner_b[part])
            active[ring, row * tokens : row * tokens + tokens, :] = act.astype(BF16)
            slope[ring, row * tokens : row * tokens + tokens, :] = der.astype(BF16)
        for copy in part_saves(part):
            copy.start()
        return carry

    inner_load(0).start()
    lax.fori_loop(0, FF_PARTS, feed, 0)
    for part in (FF_PARTS - 2, FF_PARTS - 1):
        for copy in part_saves(part):
            copy.wait()
    finish_slots(slots)
    for tail in tails:
        pl.when(has_next)(tail.wait_send)
    for copy in saves:
        copy.wait()


def encode(hidden, key_ids, query_ids, vectors, wq, wk, wv, wo, inner, outer):
    rows, tokens, width = hidden.shape
    window = tokens + SEGMAX
    hbm = pl.BlockSpec(memory_space=pltpu.HBM)
    vmem = pl.BlockSpec(memory_space=pltpu.VMEM)
    lead = lambda a: a.reshape((1, 1, 1, 1) + a.shape)
    block = wq.shape
    own, wide = (rows, tokens, width), (rows, window, width)
    return pl.pallas_call(
        encode_kernel,
        out_shape=[
            jax.ShapeDtypeStruct(own, BF16),
            jax.ShapeDtypeStruct(wide, BF16),
            jax.ShapeDtypeStruct(wide, BF16),
            jax.ShapeDtypeStruct(wide, BF16),
            jax.ShapeDtypeStruct((4,) + GRID + block, BF16),
            jax.ShapeDtypeStruct(own, BF16),
            jax.ShapeDtypeStruct(own, F32),
            jax.ShapeDtypeStruct(own, BF16),
            jax.ShapeDtypeStruct(GRID + inner.shape, BF16),
            jax.ShapeDtypeStruct(GRID + outer.shape, BF16),
            jax.ShapeDtypeStruct((rows * tokens, inner.shape[1]), BF16),
            jax.ShapeDtypeStruct((rows * tokens, inner.shape[1]), BF16),
            jax.ShapeDtypeStruct((rows, width // PAIR, 8, tokens), F32),
            jax.ShapeDtypeStruct((rows, tokens, 1), F32),
            jax.ShapeDtypeStruct((16, width), F32),
        ],
        in_specs=[hbm] + [vmem] * 11 + [hbm] * 6,
        out_specs=[hbm] * 12 + [vmem] * 3,
        scratch_shapes=[
            pltpu.VMEM((4,) + GRID + block, BF16),
            pltpu.VMEM((1, 1, 1, 1, 16, 128), BF16),
            pltpu.VMEM(GRID + (16, 128), BF16),
            pltpu.VMEM(wide, BF16),
            pltpu.VMEM(own, BF16),
            pltpu.VMEM(wide, BF16),
            pltpu.VMEM(wide, BF16),
            pltpu.VMEM(own, BF16),
            pltpu.VMEM(own, F32),
            pltpu.VMEM(own, BF16),
            pltpu.VMEM((window, tokens), F32),
            pltpu.VMEM((2,) + PIECE, BF16),
            pltpu.VMEM((4, 1, 1, 1, 1) + block, BF16),
            pltpu.VMEM((1, 1, 1, 1) + inner.shape, BF16),
            pltpu.VMEM((1, 1, 1, 1) + outer.shape, BF16),
            pltpu.VMEM((FF_PARTS, 1, PART), F32),
            pltpu.VMEM((2, rows * tokens, PART), BF16),
            pltpu.VMEM((2, rows * tokens, PART), BF16),
            pltpu.SemaphoreType.DMA((57, 8)),
            pltpu.SemaphoreType.DMA((57, 8)),
            pltpu.SemaphoreType.DMA((2, 4)),
            pltpu.SemaphoreType.DMA((24,)),
            pltpu.SemaphoreType.DMA((2, 2)),
            pltpu.SemaphoreType.DMA((9,)),
        ],
        compiler_params=pltpu.CompilerParams(collective_id=0, has_side_effects=True, vmem_limit_bytes=VMEM),
        name="gather_encode",
    )(
        hidden, key_ids, query_ids, *[v.reshape(1, -1) for v in vectors],
        lead(wq), lead(wk), lead(wv), lead(wo), lead(inner), lead(outer),
    )


def forward_kernel(active, outer, unit, cot, vec, layer_out, og, grad_second, sums, total):
    step = pl.program_id(0)
    tokens = active.shape[0]

    @pl.when(step < FF_PARTS)
    def _():
        w2 = outer[...].reshape(PART, -1)
        for start in range(0, tokens, 512):
            rows = pl.ds(start, 512)
            out = dot(active[rows, :], w2)

            @pl.when(step == 0)
            def _():
                total[rows, :] = out

            @pl.when(step > 0)
            def _():
                total[rows, :] += out

    @pl.when(step == FF_PARTS)
    def _():
        sums[...] = jnp.zeros_like(sums)

    @pl.when(step >= FF_PARTS)
    def _():
        first = pl.multiple_of((step - FF_PARTS) * 256, 256)
        for start in range(0, 256, 128):
            rows = pl.ds(start, 128)
            normed = unit[rows, :] * vec[3:4, :] + vec[4:5, :]
            centered, scale = layer_norm(total[pl.ds(first + start, 128), :] + normed + vec[5:6, :])
            layer_out[rows, :] = (centered * vec[6:7, :] + vec[7:8, :]).astype(BF16)
            up = cot[rows, :].astype(F32)
            grad = layer_norm_back(up * vec[6:7, :], centered, scale)
            grad_second[rows, :] = grad
            rounded = grad.astype(BF16)
            og[rows, :] = rounded
            sums[0:1, :] += jnp.sum(rounded.astype(F32), axis=0, keepdims=True)
            sums[1:2, :] += jnp.sum(up * centered, axis=0, keepdims=True)
            sums[2:3, :] += jnp.sum(up, axis=0, keepdims=True)


def feed_forward(active, outer, unit, cot, vec):
    tokens, width = unit.shape
    first = lambda s: jnp.minimum(s, FF_PARTS - 1)
    second = lambda s: jnp.maximum(s - FF_PARTS, 0)
    whole = lambda shape: pl.BlockSpec(shape, lambda s: (0,) * len(shape))
    rows = pl.BlockSpec((256, width), lambda s: (second(s), 0))
    return pl.pallas_call(
        forward_kernel,
        grid=(FF_PARTS + tokens // 256,),
        out_shape=[
            jax.ShapeDtypeStruct((tokens, width), BF16),
            jax.ShapeDtypeStruct((tokens, width), BF16),
            jax.ShapeDtypeStruct((tokens, width), F32),
            jax.ShapeDtypeStruct((8, width), F32),
        ],
        in_specs=[
            pl.BlockSpec((tokens, PART), lambda s: (0, first(s))),
            pl.BlockSpec((4, outer.shape[4], width), lambda s: (first(s), 0, 0)),
            rows, rows, whole(vec.shape),
        ],
        out_specs=[rows, rows, rows, whole((8, width))],
        scratch_shapes=[pltpu.VMEM((tokens, width), F32)],
        compiler_params=pltpu.CompilerParams(vmem_limit_bytes=VMEM),
        name="feed_forward",
    )(active, outer.reshape((32,) + outer.shape[4:]), unit, cot, vec)


def backward_kernel(
    active_in, slope, og, low, inner_w, outer_w, second_in, unit_in, scale, mixed_in, weights_in, vec,
    outer_sum, inner_sum, rest, ib_grad, first_out, gm_out, sums,
    acts, total, unit, mixed, wo, ig, stage, load_sem, save_sem, *bufs,
):
    step = pl.program_id(0)
    chunks = 4
    part = step - chunks
    tokens, width = og.shape
    place = Place()

    def store(j, half, value):
        @pl.when(j < FF_PARTS)
        def _():
            for group in range(4):
                outer_sum[
                    group * 32 + half * 16 : group * 32 + half * 16 + 16,
                    pl.ds(pl.multiple_of(j * 128, 128), 128),
                ] = value[:, group * 128 : group * 128 + 128]

        @pl.when(j >= FF_PARTS)
        def _():
            columns = pl.ds(pl.multiple_of((j - FF_PARTS) * PART, PART), PART)
            inner_sum[half * 16 : half * 16 + 16, columns] = value

    queue = Sums(place, FF_PARTS + EARLY, stage, lambda j: lax.rem(j, FF_PARTS), bufs, store)
    loads = [
        pltpu.make_async_copy(source, target, load_sem.at[number])
        for number, (source, target) in enumerate(
            ((active_in, acts), (second_in, total), (unit_in, unit), (mixed_in, mixed), (weights_in.at[3], wo))
        )
    ]

    def keep(number):
        return pltpu.make_async_copy(
            stage.at[number + EARLY if number < FF_PARTS - EARLY else number - FF_PARTS + EARLY],
            rest.at[number],
            save_sem.at[number],
        )

    @pl.when(step == 0)
    def _():
        for load in loads:
            load.start()
        meet(place)
        loads[0].wait()

    @pl.when(step < chunks)
    def _():
        right = og[:, pl.ds(pl.multiple_of(step * 256, 256), 256)]
        for y in range(2):
            for x in range(2):
                first = (y * 2 + x) * 1024
                grad = dot_tn(acts[:, first : first + 1024], right).astype(BF16).reshape(4, 2, 4, 32, 256)
                for piece in range(2):
                    for group in range(4):
                        stage[2 * step + piece, y, x, :, :, :, group * 128 : group * 128 + 128] = grad[
                            :, :, group, :, piece * 128 : piece * 128 + 128
                        ]
        queue.tick(step)

    @pl.when(step >= chunks)
    def _():
        w1 = inner_w[...].reshape(width, PART)
        w2 = outer_w[...].reshape(PART, width)
        ib_grad[...] = jnp.zeros_like(ib_grad)
        for start in range(0, tokens, 512):
            rows = pl.ds(start, 512)
            piece = (dot_nt(og[rows, :], w2) * slope[rows, :].astype(F32)).astype(BF16)
            ig[rows, :] = piece
            ib_grad[0] += jnp.sum(piece.astype(F32), axis=0, keepdims=True)
        beat = chunks + lax.div(3 * part, 2)
        odd = lax.rem(part, 2)
        pl.when(odd == 1)(functools.partial(queue.tick, beat))
        stage[part] = dot_tn(low[...], ig[...]).astype(BF16).reshape(PIECE)
        for number in range(FF_PARTS - EARLY):
            pl.when(part == EARLY + number)(lambda number=number: keep(number).start())
        queue.tick(beat + odd)
        pl.when(part == 0)(loads[1].wait)
        for start in range(0, tokens, 512):
            rows = pl.ds(start, 512)
            total[rows, :] += dot_nt(ig[rows, :], w1)

    @pl.when(step == pl.num_programs(0) - 1)
    def _():
        for load in loads[2:]:
            load.wait()
        sums[...] = jnp.zeros_like(sums)
        matrix = wo[...].reshape(width, width)
        for start in range(0, tokens, 256):
            rows = pl.ds(start, 256)
            up = total[rows, :]
            centered = unit[rows, :]
            grad = layer_norm_back(up * vec[3:4, :], centered, scale[rows, :])
            total[rows, :] = grad
            rounded = grad.astype(BF16)
            acts[rows, :width] = rounded
            sums[0:1, :] += jnp.sum(rounded.astype(F32), axis=0, keepdims=True)
            sums[1:2, :] += jnp.sum(up * centered, axis=0, keepdims=True)
            sums[2:3, :] += jnp.sum(up, axis=0, keepdims=True)
            acts[rows, width : 2 * width] = dot_nt(rounded, matrix).astype(BF16)
            queue.tick(16 + start // 256)
        save_first = pltpu.make_async_copy(total, first_out, load_sem.at[0])
        save_gm = pltpu.make_async_copy(acts.at[:, pl.ds(width, width)], gm_out, load_sem.at[1])
        save_first.start()
        save_gm.start()
        for piece in range(2):
            columns = slice(piece * PART, piece * PART + PART)
            stage[piece] = dot_tn(mixed[...], acts[:, columns]).astype(BF16).reshape(PIECE)
            keep(FF_PARTS - EARLY + piece).start()
        save_first.wait()
        save_gm.wait()
        for number in range(FF_PARTS - EARLY + 2):
            keep(number).wait()
        queue.finish()


def feed_backward(active, slope, og, low, inner, outer, grad_second, unit, scale, mixed, weights, vec):
    tokens, width = og.shape
    part = lambda s: jnp.maximum(s - 4, 0)
    whole = lambda shape: pl.BlockSpec(shape, lambda s: (0,) * len(shape), pipeline_mode=pl.Buffered(1))
    kept = lambda shape: pl.BlockSpec(shape, lambda s: (0,) * len(shape))
    hbm = pl.BlockSpec(memory_space=pltpu.HBM)
    count = FF_PARTS + EARLY
    rest = FF_PARTS - EARLY + 2
    return pl.pallas_call(
        backward_kernel,
        grid=(4 + FF_PARTS,),
        out_shape=[
            jax.ShapeDtypeStruct(outer.shape[4:], F32),
            jax.ShapeDtypeStruct((32, EARLY * PART), F32),
            jax.ShapeDtypeStruct((rest,) + PIECE, BF16),
            jax.ShapeDtypeStruct((FF_PARTS, 1, PART), F32),
            jax.ShapeDtypeStruct((tokens, width), F32),
            jax.ShapeDtypeStruct((tokens, width), BF16),
            jax.ShapeDtypeStruct((8, width), F32),
        ],
        in_specs=[
            hbm, pl.BlockSpec((tokens, PART), lambda s: (0, part(s))), whole(og.shape), whole(low.shape),
            pl.BlockSpec(GRID + (32, PART), lambda s: (0, 0, 0, 0, 0, part(s))),
            pl.BlockSpec((4, outer.shape[4], width), lambda s: (part(s), 0, 0)),
            hbm, hbm, whole(scale.shape), hbm, hbm, whole(vec.shape),
        ],
        out_specs=[
            kept(outer.shape[4:]), kept((32, EARLY * PART)), hbm,
            pl.BlockSpec((1, 1, PART), lambda s: (part(s), 0, 0)), hbm, hbm, kept((8, width)),
        ],
        scratch_shapes=[
            pltpu.VMEM((tokens, FF_PARTS * PART), BF16),
            pltpu.VMEM((tokens, width), F32),
            pltpu.VMEM((tokens, width), F32),
            pltpu.VMEM((tokens, width), BF16),
            pltpu.VMEM(GRID + (32, width), BF16),
            pltpu.VMEM((tokens, PART), BF16),
            pltpu.VMEM((FF_PARTS,) + PIECE, BF16),
            pltpu.SemaphoreType.DMA((5,)),
            pltpu.SemaphoreType.DMA((rest,)),
        ]
        + sums_buffers(count),
        compiler_params=pltpu.CompilerParams(
            collective_id=3, has_side_effects=True, vmem_limit_bytes=VMEM
        ),
        name="feed_backward",
    )(
        active, slope, og, low, inner, outer.reshape((32,) + outer.shape[4:]), grad_second, unit, scale, mixed,
        weights, vec,
    )


LATE = FF_PARTS - EARLY + 2
BACK = LATE + 4


def attend_back_kernel(
    q, k, v, gm, mixed, lse, key_ids, query_ids, xt, rest, inner_early,
    dq_out, dk_out, dv_out, tail_out, sums, inner_sum, wo_sum, qkv_sum,
    bias, dq_all, dk_all, dv_all, dk_sum, dv_sum, stage, load_sem, *bufs,
):
    group, row, inner = pl.program_id(0), pl.program_id(1), pl.program_id(2)
    step = group * 4 + row * 2 + inner
    tokens = q.shape[1]
    place = Place()

    def load(j):
        return pltpu.make_async_copy(rest.at[j], stage.at[j], load_sem.at[j])

    def ready(j):
        pl.when(j < LATE)(lambda: load(j).wait())

    def store(j, half, value):
        rows = slice(half * 16, half * 16 + 16)
        for number in range(FF_PARTS - EARLY):

            @pl.when(j == number)
            def _():
                first = (EARLY + number) * PART
                inner_sum[rows, first : first + PART] = value

        for piece in range(2):

            @pl.when(j == LATE - 2 + piece)
            def _():
                wo_sum[rows, piece * PART : piece * PART + PART] = value

        @pl.when(j >= LATE)
        def _():
            qkv_sum[j - LATE, rows, :] = value

    def order(beat):
        j = jnp.where(beat <= LATE, beat, jnp.where(beat <= 8, beat - 7 + LATE + 1, LATE + 3))
        return j, ((beat >= 0) & (beat <= LATE)) | (beat == 7) | (beat == 8) | (beat == 11)

    queue = Sums(place, BACK, stage, lambda j: j, bufs, store, ready=ready, order=order)

    @pl.when(step == 0)
    def _():
        for j in range(LATE):
            load(j).start()
        meet(place)
        inner_sum[:, : EARLY * PART] = inner_early[...]

    @pl.when((group == 0) & (inner == 0))
    def _():
        bias[row] = mask_scores(key_ids[0], query_ids[0])

    k_t = k[0].T
    for start, (low_key, high_key) in zip(range(0, tokens, BLOCK), key_ranges(tokens)):
        rows = slice(start, start + BLOCK)
        both_q, both_g = both_heads(q[0, rows, :]), both_heads(gm[0, rows, :])
        product = (gm[0, rows, :].astype(F32) * mixed[0, rows, :].astype(F32)).T
        delta = jnp.concatenate(
            [jnp.sum(product[head * HD : head * HD + HD, :], axis=0, keepdims=True) for head in range(2)], axis=1
        )
        logs = jnp.concatenate([lse[0, 0, head : head + 1, rows] for head in range(2)], axis=1)
        mask = bias[row, low_key:high_key, rows]
        s = dot_nt(k[0, low_key:high_key, :], both_q) * SCORE_SCALE + jnp.concatenate([mask, mask], axis=1)
        probs = jnp.exp2(s - logs)
        dprob = dot_nt(v[0, low_key:high_key, :], both_g)
        score_grad = (probs * (dprob - delta)).astype(BF16)
        dv = dot(probs.astype(BF16), both_g)
        dk = dot(score_grad, both_q)
        dq_out[0, rows, :] = (own_heads(dot(k_t[:, low_key:high_key], score_grad)) * 0.125).T.astype(BF16)
        if start == 0:
            dk_sum[low_key:high_key, :] = dk
            dv_sum[low_key:high_key, :] = dv
            dk_sum[high_key:, :] = jnp.zeros((dk_sum.shape[0] - high_key, PAIR), F32)
            dv_sum[high_key:, :] = jnp.zeros((dk_sum.shape[0] - high_key, PAIR), F32)
        else:
            dk_sum[low_key:high_key, :] += dk
            dv_sum[low_key:high_key, :] += dv
    dk_out[0] = (dk_sum[...] * 0.125).astype(BF16)
    dv_out[0] = dv_sum[...].astype(BF16)
    columns = pl.ds(pl.multiple_of(inner * PAIR, PAIR), PAIR)
    dq_all[row, :, columns] = dq_out[0]
    dk_all[row, :, columns] = dk_out[0]
    dv_all[row, :, columns] = dv_out[0]

    @pl.when((row == 1) & (inner == 1))
    def _():
        span = 2 * PAIR
        pair_slot = jnp.where(group == 3, BACK, jnp.where(group == 2, LATE + 3, LATE + group))
        value_slot = jnp.where(group < 2, LATE + 2, BACK + 1)
        value_half = pl.ds(pl.multiple_of(lax.rem(group, 2) * span, span), span)
        for number, source in enumerate((dq_all, dk_all, dv_all)):
            first = SEGMAX if number == 0 else 0
            grad = dot_tn(xt[0, first:, :], source[0]) + dot_tn(xt[1, first:, :], source[1])
            grad = grad.astype(BF16).reshape(GRID + (32, span))
            if number < 2:
                stage[pair_slot, :, :, :, :, :, number * span : number * span + span] = grad
            else:
                stage[value_slot, :, :, :, :, :, value_half] = grad
        sums[...] = jnp.zeros_like(sums)
        for number, source in enumerate((dq_all, dv_all)):
            added = jnp.sum(source[0].astype(F32), axis=0, keepdims=True) + jnp.sum(
                source[1].astype(F32), axis=0, keepdims=True
            )
            sums[number : number + 1, :] = added

    queue.tick(step)

    @pl.when(step == 15)
    def _():
        saves = [pltpu.make_async_copy(stage.at[BACK + n], tail_out.at[n], load_sem.at[n]) for n in range(2)]
        for save in saves:
            save.start()
        for beat in range(16, 19):
            queue.tick(beat)
        queue.finish()
        for save in saves:
            save.wait()


def attend_back(q, k, v, gm, mixed, lse, key_ids, query_ids, xt, rest, inner_early):
    rows, tokens, width = q.shape
    window = k.shape[1]
    groups = width // (2 * PAIR)
    whole = lambda shape: pl.BlockSpec(shape, lambda g, r, i: (0,) * len(shape), pipeline_mode=pl.Buffered(1))
    kept = lambda shape: pl.BlockSpec(shape, lambda g, r, i: (0,) * len(shape))
    per_pair = lambda n: pl.BlockSpec((1, n, PAIR), lambda g, r, i: (r, 0, g * 2 + i))
    per_row = lambda *s: pl.BlockSpec((1,) + s, lambda g, r, i: (r, 0, 0))
    hbm = pl.BlockSpec(memory_space=pltpu.HBM)
    return pl.pallas_call(
        attend_back_kernel,
        grid=(groups, rows, 2),
        out_shape=[
            jax.ShapeDtypeStruct((rows, tokens, width), BF16),
            jax.ShapeDtypeStruct((rows, window, width), BF16),
            jax.ShapeDtypeStruct((rows, window, width), BF16),
            jax.ShapeDtypeStruct((2,) + PIECE, BF16),
            jax.ShapeDtypeStruct((8, width), F32),
            jax.ShapeDtypeStruct((32, FF_PARTS * PART), F32),
            jax.ShapeDtypeStruct((32, width), F32),
            jax.ShapeDtypeStruct((4, 32, PART), F32),
        ],
        in_specs=[
            per_pair(tokens), per_pair(window), per_pair(window), per_pair(tokens), per_pair(tokens),
            pl.BlockSpec((1, 1, 8, tokens), lambda g, r, i: (r, g * 2 + i, 0, 0)),
            per_row(window, 1), per_row(1, tokens), whole(xt.shape), hbm, whole(inner_early.shape),
        ],
        out_specs=[
            per_pair(tokens), per_pair(window), per_pair(window), hbm,
            pl.BlockSpec((8, 2 * PAIR), lambda g, r, i: (0, g)),
            kept((32, FF_PARTS * PART)), kept((32, width)), kept((4, 32, PART)),
        ],
        scratch_shapes=[
            pltpu.VMEM((rows, window, tokens), F32),
            pltpu.VMEM((rows, tokens, 2 * PAIR), BF16),
            pltpu.VMEM((rows, window, 2 * PAIR), BF16),
            pltpu.VMEM((rows, window, 2 * PAIR), BF16),
            pltpu.VMEM((window, PAIR), F32),
            pltpu.VMEM((window, PAIR), F32),
            pltpu.VMEM((BACK + 2,) + PIECE, BF16),
            pltpu.SemaphoreType.DMA((LATE,)),
        ]
        + sums_buffers(BACK),
        compiler_params=pltpu.CompilerParams(
            collective_id=4, has_side_effects=True, vmem_limit_bytes=VMEM
        ),
        name="attend_back",
    )(q, k, v, gm, mixed, lse, key_ids, query_ids, xt, rest, inner_early)


def shards(vector, base, shift):
    count = vector.shape[1]
    device = lax.broadcasted_iota(jnp.int32, (32, count), 0)
    column = lax.broadcasted_iota(jnp.int32, (32, count), 1)
    rows = jnp.where(device == column >> shift, vector, 0.0).astype(BF16)
    lane = lax.broadcasted_iota(jnp.int32, (count, 128), 1)
    place = lax.broadcasted_iota(jnp.int32, (count, 128), 0)
    pick = jnp.where(lane == base + (place & (2**shift - 1)), 1.0, 0.0).astype(BF16)
    return dot(rows, pick)


def finish_kernel(
    tail_in, sums0, sums1, sums2, ib_grad, qkv_early, dq_in, dk_in, dv_in, weights_in, first_in,
    query_sum, key_sum, value_sum, small_sum, gh_out, tail_there,
    dq, dk, dv, weights, gh, tail_here, stage, small_stage, load_sem, tail_sem, *bufs,
):
    place = Place()
    loads = [
        pltpu.make_async_copy(source, target, load_sem.at[number])
        for number, (source, target) in enumerate(
            (
                (tail_in, stage),
                (weights_in.at[pl.ds(0, 3)], weights),
                (dk_in, dk),
                (dv_in, dv),
                (dq_in, dq),
                (first_in, gh),
            )
        )
    ]
    for load in loads:
        load.start()
    meet(place, -1)
    span = 2 * PAIR

    def store(j, half, value):
        rows = slice(half * 16, half * 16 + 16)
        if j == 0:
            query_sum[rows, 3 * span :] = value[:, :span]
            key_sum[rows, 3 * span :] = value[:, span:]
        else:
            value_sum[rows, 2 * span :] = value

    def store_small(j, half, value):
        small_sum[...] = value

    beats = (0, 1, 2, 3, 4)
    queue = Sums(place, 2, stage, lambda j: j, bufs[:6], store, offsets=beats)
    small = Sums(place, 1, small_stage, lambda j: j, bufs[6:], store_small, halves=1, offsets=beats)
    loads[0].wait()
    queue.tick(0)
    tokens, width = dq.shape[1], dq.shape[2]
    for load in loads[1:4]:
        load.wait()
    matrix = [weights.at[m] for m in range(3)]
    send_tail, recv_tail = place.seq > 0, place.seq < 7
    tails = [
        remote(
            tail_here.at[row], tail_there.at[row], tail_sem.at[0, row], tail_sem.at[1, row],
            place.device(z=lax.rem(place.z + 3 + place.c, 4), c=1 - place.c),
        )
        for row in range(2)
    ]
    for row in range(2):
        tail_here[row] = (
            dot_nt(dk[row, :SEGMAX, :], matrix[1][...].reshape(width, width))
            + dot_nt(dv[row, :SEGMAX, :], matrix[2][...].reshape(width, width))
        ).astype(BF16)
        pl.when(send_tail)(tails[row].start)
        if row == 0:
            queue.tick(1)
    packed = []
    vectors = [sums0[0:1], sums0[1:2], sums1[0:1], sums1[1:2], sums1[2:3], sums2[0:1], sums2[1:2], sums2[2:3]]
    for first in (0, 4):
        packed.append(sum(shards(vectors[first + n], n * 32, 5) for n in range(4)))
    inner = [ib_grad[part][:, n * 128 : n * 128 + 128] for part in range(FF_PARTS) for n in range(4)]
    packed.append(jnp.concatenate(inner, axis=0))
    packed = [p.astype(BF16).astype(F32) for p in packed]
    at = lax.broadcasted_iota(jnp.int32, (32, 16, 128), 1)
    block = jnp.zeros((32, 16, 128), F32)
    for number, value in enumerate(packed):
        block = jnp.where(at == number, jnp.broadcast_to(value[:, None, :], (32, 16, 128)), block)
    small_stage[0] = block.astype(BF16).reshape(GRID + (16, 128))

    small.tick(0)
    queue.tick(2)
    small.tick(1)
    for load in loads[4:]:
        load.wait()

    def own_rows(row):
        for column in range(0, width, 512):
            cols = slice(column, column + 512)
            total = gh[row, :, cols]
            for number, (source, first) in enumerate(((dq, 0), (dk, SEGMAX), (dv, SEGMAX))):
                part = weights[number, column // 512]
                total = total + dot_nt(source[row, first:, :], part.reshape(512, width))
            gh[row, :, cols] = total

    own_rows(0)
    queue.tick(3)
    small.tick(2)
    own_rows(1)
    save = pltpu.make_async_copy(gh, gh_out, load_sem.at[0])
    save.start()
    query_sum[:, : 3 * span] = jnp.concatenate([qkv_early[n, :, :span] for n in (0, 1, 3)], axis=1)
    key_sum[:, : 3 * span] = jnp.concatenate([qkv_early[n, :, span:] for n in (0, 1, 3)], axis=1)
    value_sum[:, : 2 * span] = qkv_early[2]
    for beat in (4, 5):
        queue.tick(beat)
        small.tick(beat - 1)
    queue.finish()
    small.finish()

    @pl.when(place.seq == 7)
    def _():
        tail_there[...] = jnp.zeros_like(tail_there)

    for tail in tails:
        pl.when(recv_tail)(tail.wait_recv)
        pl.when(send_tail)(tail.wait_send)
    save.wait()


def finish(tail_in, sums0, sums1, sums2, ib_grad, qkv_early, dq, dk, dv, weights, grad_first):
    rows, tokens, width = dq.shape
    hbm = pl.BlockSpec(memory_space=pltpu.HBM)
    vmem = pl.BlockSpec(memory_space=pltpu.VMEM)
    return pl.pallas_call(
        finish_kernel,
        out_shape=[
            jax.ShapeDtypeStruct((32, width), F32),
            jax.ShapeDtypeStruct((32, width), F32),
            jax.ShapeDtypeStruct((32, width), F32),
            jax.ShapeDtypeStruct((16, 128), F32),
            jax.ShapeDtypeStruct((rows, tokens, width), F32),
            jax.ShapeDtypeStruct((rows, SEGMAX, width), BF16),
        ],
        in_specs=[hbm] + [vmem] * 5 + [hbm] * 5,
        out_specs=[vmem] * 4 + [hbm, vmem],
        scratch_shapes=[
            pltpu.VMEM(dq.shape, BF16),
            pltpu.VMEM(dk.shape, BF16),
            pltpu.VMEM(dv.shape, BF16),
            pltpu.VMEM((3,) + weights.shape[1:], BF16),
            pltpu.VMEM((rows, tokens, width), F32),
            pltpu.VMEM((rows, SEGMAX, width), BF16),
            pltpu.VMEM((2,) + PIECE, BF16),
            pltpu.VMEM((1,) + GRID + (16, 128), BF16),
            pltpu.SemaphoreType.DMA((6,)),
            pltpu.SemaphoreType.DMA((2, 2)),
        ]
        + sums_buffers(2)
        + sums_buffers(1, 128, 1),
        compiler_params=pltpu.CompilerParams(
            collective_id=5, has_side_effects=True, vmem_limit_bytes=VMEM
        ),
        name="sum_gradients",
    )(tail_in, sums0, sums1, sums2, ib_grad, qkv_early, dq, dk, dv, weights, grad_first)


def deliver_kernel(gh, returned, *refs):
    count = len(refs) // 2
    sources, out, targets = refs[:count], refs[count], refs[count + 1 :]
    late = lax.rem(pl.program_id(0), 2) == 1
    out[...] = gh[...] + jnp.where(late, returned[...].astype(F32), 0.0)

    @pl.when(pl.program_id(0) == 0)
    def _():
        for source, target in zip(sources, targets):
            target[...] = source[...]


def deliver(gh, returned, arrays):
    rows, tokens, width = gh.shape
    whole = lambda a: pl.BlockSpec(a.shape, lambda s: (0,) * a.ndim)
    block = pl.BlockSpec((1, SEGMAX, width), lambda s: (s // 2, s % 2, 0))
    back = pl.BlockSpec((1, SEGMAX, width), lambda s: (s // 2, 0, 0))
    return pl.pallas_call(
        deliver_kernel,
        grid=(2 * rows,),
        out_shape=[jax.ShapeDtypeStruct(gh.shape, F32)] + [jax.ShapeDtypeStruct(a.shape, a.dtype) for a in arrays],
        in_specs=[block, back] + [whole(a) for a in arrays],
        out_specs=[block] + [whole(a) for a in arrays],
        compiler_params=pltpu.CompilerParams(vmem_limit_bytes=VMEM),
        name="deliver",
    )(gh, returned, *arrays)


def local(
    hidden_in, segment_ids, query_weight, query_bias, key_weight, value_weight, value_bias, output_weight,
    output_bias, first_gain, first_shift, inner_weight, inner_bias, outer_weight, outer_bias, second_gain,
    second_shift, cotangent,
):
    rows, tokens, width = hidden_in.shape
    window = tokens + SEGMAX
    vectors = (query_bias, value_bias, output_bias, first_gain, first_shift, outer_bias, second_gain, second_shift, inner_bias)
    padded = jnp.concatenate([jnp.full((rows, SEGMAX), -1, jnp.int32), segment_ids], axis=1)
    key_ids = lax.dynamic_slice_in_dim(padded, lax.axis_index("seq") * tokens, window, 1)
    query_ids = key_ids[:, None, SEGMAX:]
    key_ids = key_ids[:, :, None]
    q, k, v, xt, weights, mixed, unit, low, inner, outer, active, slope, lse, scale, vec = encode(
        hidden_in, key_ids, query_ids, vectors, query_weight, key_weight, value_weight, output_weight,
        inner_weight, outer_weight,
    )
    flat = lambda a: a.reshape(rows * tokens, a.shape[-1])
    layer_out, og, grad_second, sums2 = feed_forward(active, outer, flat(unit), flat(cotangent), vec)
    outer_sum, inner_early, rest, ib_grad, grad_first, gm, sums1 = feed_backward(
        active, slope, og, flat(low), inner, outer, grad_second, flat(unit), flat(scale), flat(mixed), weights, vec
    )
    dq, dk, dv, tail, sums0, inner_sum, wo_sum, qkv_early = attend_back(
        q, k, v, gm.reshape(rows, tokens, width), mixed, lse, key_ids, query_ids, xt, rest, inner_early
    )
    query_sum, key_sum, value_sum, small_sum, grad_hidden, returned = finish(
        tail, sums0, sums1, sums2, ib_grad, qkv_early, dq, dk, dv, weights, grad_first.reshape(rows, tokens, width)
    )
    grad_hidden, query_sum, key_sum, value_sum, wo_sum, inner_sum, outer_sum, small_sum = deliver(
        grad_hidden, returned, (query_sum, key_sum, value_sum, wo_sum, inner_sum, outer_sum, small_sum)
    )
    vector = small_sum[:2].reshape(8, 32)
    return (
        layer_out.reshape(rows, tokens, width),
        grad_hidden,
        query_sum,
        vector[0],
        key_sum,
        value_sum,
        vector[1],
        wo_sum,
        vector[2],
        vector[3],
        vector[4],
        inner_sum,
        small_sum[2],
        outer_sum,
        vector[5],
        vector[6],
        vector[7],
    )


def solution(mesh):
    in_specs = (
        P("dp", "seq", None),
        P("dp", None),
        P(("dp", "seq"), None),
        P(("dp", "seq")),
        P(("dp", "seq"), None),
        P(("dp", "seq"), None),
        P(("dp", "seq")),
        P(("dp", "seq"), None),
        P(("dp", "seq")),
        P(("dp", "seq")),
        P(("dp", "seq")),
        P(("dp", "seq"), None),
        P(("dp", "seq")),
        P(("dp", "seq"), None),
        P(("dp", "seq")),
        P(("dp", "seq")),
        P(("dp", "seq")),
        P("dp", "seq", None),
    )
    out_specs = (
        P("dp", "seq", None),
        P("dp", "seq", None),
        P(("dp", "seq"), None),
        P(("dp", "seq")),
        P(("dp", "seq"), None),
        P(("dp", "seq"), None),
        P(("dp", "seq")),
        P(("dp", "seq"), None),
        P(("dp", "seq")),
        P(("dp", "seq")),
        P(("dp", "seq")),
        P(("dp", "seq"), None),
        P(("dp", "seq")),
        P(("dp", "seq"), None),
        P(("dp", "seq")),
        P(("dp", "seq")),
        P(("dp", "seq")),
    )
    fits = dict(mesh.shape) == {"dp": 4, "seq": 8}
    body = local if fits else plain
    return jax.shard_map(body, mesh=mesh, in_specs=in_specs, out_specs=out_specs, check_vma=False)
```

profile of v0, /device:TPU:0, one launch (start us, length us, event | category | flops | bytes accessed | tf_op | source)
XLA Modules:
  0.0 362.4 jit_solution(1283640951411240665)
XLA Ops:
  0.7 0.7 pad_dynamic-slice_fusion
  1.4 0.6 broadcast_in_dim.8.query_ids
  2.0 0.7 fusion
  2.6 1.3 copy.35.key_ids
  3.9 145.8 %gather_encode.1 = (bf16[2,512,1024]{2,1,0:T(8,128)(2,1)}, bf16[2,768,1024]{2,1,0:T(8,128)(2,1)}, bf16[2,768,1024]{2,1,0:T(8,128)(2,1)}, bf16[2,768,1024]{2,1,0:...) custom-call(bf16[2,512,1024]{2,1,0:T(8,128)(2,1)} %x_in.1, ...), custom_call_target="tpu_custom_call" | custom-call | tf_op jit(solution)/shard_map/gather_encode/pallas_call | solution.py:934
  149.7 24.4 %feed_forward.1 = (bf16[1024,1024]{1,0:T(8,128)(2,1)}, bf16[1024,1024]{1,0:T(8,128)(2,1)}, f32[1024,1024]{1,0:T(8,128)}, f32[8,1024]{1,0:T(8,128)}) custom-call(bf16[1024,4096]{1,0:T(8,128)(2,1)} %get-tuple-element.65.active.active_in, bf16[32,128,1024]{2,1,0:T(8,128)(2,1)} %bitcast.44, f32[1024,1024]{1,0:T(8,128)} %bitcast.46, bf16[1024,1024]{1,0:T(8,128)(2,1)} %bitcast.52, ...), custom_call_target="tpu_custom_call" | custom-call | tf_op jit(solution)/shard_map/feed_forward/pallas_call | solution.py:1036
  174.1 85.0 %feed_backward.1 = (f32[128,1024]{1,0:T(8,128)}, f32[32,2560]{1,0:T(8,128)}, bf16[5,2,2,4,2,32,512]{6,5,4,3,2,1,0:T(8,128)(2,1)}, f32[8,1,512]{2,1,0:T(1,128)}, ...) custom-call(bf16[1024,4096]{1,0:T(8,128)(2,1)} %get-tuple-element.65.active.active_in, ...), custom_call_target="tpu_custom_call" | custom-call | tf_op jit(solution)/shard_map/feed_backward/pallas_call | solution.py:1182
  259.1 64.3 %attend_back.1 = (bf16[2,512,1024]{2,1,0:T(8,128)(2,1)}, bf16[2,768,1024]{2,1,0:T(8,128)(2,1)}, bf16[2,768,1024]{2,1,0:T(8,128)(2,1)}, bf16[2,2,2,4,2,32,512]{6,...) custom-call(bf16[2,512,1024]{2,1,0:T(8,128)(2,1)} %get-tuple-element, ...), custom_call_target="tpu_custom_call" | custom-call | tf_op jit(solution)/shard_map/attend_back/pallas_call | solution.py:1358
  323.4 30.1 %sum_gradients.1 = (f32[32,1024]{1,0:T(8,128)}, f32[32,1024]{1,0:T(8,128)}, f32[32,1024]{1,0:T(8,128)}, f32[16,128]{1,0:T(8,128)}, f32[2,512,1024]{2,1,0:T(8,128)}, /*index=5*/bf16[2,256,1024]{2,1,0:T(8,128)(2,1)}) custom-call(bf16[2,2,2,4,2,32,512]{6,5,4,3,2,1,0:T(8,128)(2,1)} %get-tuple-element.86.tail_in, f32[8,1024]{1,0:T(8,128)} %get-tuple-element.87.sums0, ...), custom_call_target="tpu_custom_call" | custom-call | tf_op jit(solution)/shard_map/sum_gradients/pallas_call | solution.py:1527
  353.5 6.2 %deliver.1 = (f32[2,512,1024]{2,1,0:T(8,128)}, f32[32,1024]{1,0:T(8,128)}, f32[32,1024]{1,0:T(8,128)}, f32[32,1024]{1,0:T(8,128)}, f32[32,1024]{1,0:T(8,128)}, /...) custom-call(f32[2,512,1024]{2,1,0:T(8,128)} %get-tuple-element.96.gh, ...), custom_call_target="tpu_custom_call" | custom-call | tf_op jit(solution)/shard_map/deliver/pallas_call | solution.py:1577
  359.7 1.2 slice_bitcast_fusion.3
  360.9 0.7 slice.34
  361.5 0.1 reshape.135
  361.6 0.5 slice_bitcast_fusion
where the time goes:
time: 369 us; the launch traced here: 362 us
  Pallas kernels  356 us (96%)
  local copies, waits for them, and re-layouts  5.73 us (2%)
    pallas_call x1, Pallas kernels, encode(): pl.pallas_call(encode_kernel, out_shape=[jax.ShapeDtypeStruct(own, BF16),...  146 us
    pallas_call x1, Pallas kernels, feed_backward(): pl.pallas_call(backward_kernel, grid=(4 + FF_PARTS,), out_shape=[jax.Shap...  85 us
    pallas_call x1, Pallas kernels, attend_back(): pl.pallas_call(attend_back_kernel, grid=(groups, rows, 2), out_shape=[jax...  64.3 us
    pallas_call x1, Pallas kernels, finish(): pl.pallas_call(finish_kernel, out_shape=[jax.ShapeDtypeStruct((32, width)...  30.1 us
    pallas_call x1, Pallas kernels, feed_forward(): pl.pallas_call(forward_kernel, grid=(FF_PARTS + tokens // 256,), out_shap...  24.4 us

commit v1 on v0

--- a/solution.py
+++ b/solution.py
@@ -489,8 +489,11 @@
                 copy.wait_send()
 
 
+LAGS = (0, 1, 4, 7, 9)
+
+
 class Sums:
-    def __init__(self, place, count, stage, slot, bufs, store, halves=2, ready=None, order=None, offsets=(0, 1, 3, 5, 7)):
+    def __init__(self, place, count, stage, slot, bufs, store, halves=2, ready=None, order=None, offsets=LAGS):
         self.place, self.count, self.stage, self.slot = place, count, stage, slot
         self.order, self.offsets = order, offsets
         self.r0, self.r1, self.r2, self.r3, self.send, self.recv = bufs
@@ -986,13 +989,16 @@
     )
 
 
+FORWARD = 4
+
+
 def forward_kernel(active, outer, unit, cot, vec, layer_out, og, grad_second, sums, total):
     step = pl.program_id(0)
     tokens = active.shape[0]
 
-    @pl.when(step < FF_PARTS)
+    @pl.when(step < FORWARD)
     def _():
-        w2 = outer[...].reshape(PART, -1)
+        w2 = outer[...].reshape(-1, total.shape[1])
         for start in range(0, tokens, 512):
             rows = pl.ds(start, 512)
             out = dot(active[rows, :], w2)
@@ -1005,13 +1011,13 @@
             def _():
                 total[rows, :] += out
 
-    @pl.when(step == FF_PARTS)
+    @pl.when(step == FORWARD)
     def _():
         sums[...] = jnp.zeros_like(sums)
 
-    @pl.when(step >= FF_PARTS)
+    @pl.when(step >= FORWARD)
     def _():
-        first = pl.multiple_of((step - FF_PARTS) * 256, 256)
+        first = pl.multiple_of((step - FORWARD) * 256, 256)
         for start in range(0, 256, 128):
             rows = pl.ds(start, 128)
             normed = unit[rows, :] * vec[3:4, :] + vec[4:5, :]
@@ -1029,13 +1035,13 @@
 
 def feed_forward(active, outer, unit, cot, vec):
     tokens, width = unit.shape
-    first = lambda s: jnp.minimum(s, FF_PARTS - 1)
-    second = lambda s: jnp.maximum(s - FF_PARTS, 0)
+    first = lambda s: jnp.minimum(s, FORWARD - 1)
+    second = lambda s: jnp.maximum(s - FORWARD, 0)
     whole = lambda shape: pl.BlockSpec(shape, lambda s: (0,) * len(shape))
     rows = pl.BlockSpec((256, width), lambda s: (second(s), 0))
     return pl.pallas_call(
         forward_kernel,
-        grid=(FF_PARTS + tokens // 256,),
+        grid=(FORWARD + tokens // 256,),
         out_shape=[
             jax.ShapeDtypeStruct((tokens, width), BF16),
             jax.ShapeDtypeStruct((tokens, width), BF16),
@@ -1043,8 +1049,8 @@
             jax.ShapeDtypeStruct((8, width), F32),
         ],
         in_specs=[
-            pl.BlockSpec((tokens, PART), lambda s: (0, first(s))),
-            pl.BlockSpec((4, outer.shape[4], width), lambda s: (first(s), 0, 0)),
+            pl.BlockSpec((tokens, active.shape[1] // FORWARD), lambda s: (0, first(s))),
+            pl.BlockSpec((32 // FORWARD, outer.shape[4], width), lambda s: (first(s), 0, 0)),
             rows, rows, whole(vec.shape),
         ],
         out_specs=[rows, rows, rows, whole((8, width))],
@@ -1101,8 +1107,11 @@
         meet(place)
         loads[0].wait()
 
+    beat, odd = lax.div(3 * step, 2), lax.rem(step, 2)
+
     @pl.when(step < chunks)
     def _():
+        pl.when(odd == 1)(functools.partial(queue.tick, beat))
         right = og[:, pl.ds(pl.multiple_of(step * 256, 256), 256)]
         for y in range(2):
             for x in range(2):
@@ -1113,7 +1122,7 @@
                         stage[2 * step + piece, y, x, :, :, :, group * 128 : group * 128 + 128] = grad[
                             :, :, group, :, piece * 128 : piece * 128 + 128
                         ]
-        queue.tick(step)
+        queue.tick(beat + odd)
 
     @pl.when(step >= chunks)
     def _():
@@ -1125,8 +1134,6 @@
             piece = (dot_nt(og[rows, :], w2) * slope[rows, :].astype(F32)).astype(BF16)
             ig[rows, :] = piece
             ib_grad[0] += jnp.sum(piece.astype(F32), axis=0, keepdims=True)
-        beat = chunks + lax.div(3 * part, 2)
-        odd = lax.rem(part, 2)
         pl.when(odd == 1)(functools.partial(queue.tick, beat))
         stage[part] = dot_tn(low[...], ig[...]).astype(BF16).reshape(PIECE)
         for number in range(FF_PARTS - EARLY):
@@ -1155,7 +1162,9 @@
             sums[1:2, :] += jnp.sum(up * centered, axis=0, keepdims=True)
             sums[2:3, :] += jnp.sum(up, axis=0, keepdims=True)
             acts[rows, width : 2 * width] = dot_nt(rounded, matrix).astype(BF16)
-            queue.tick(16 + start // 256)
+            queue.tick(18 + start // 256)
+        for late in range(22, FF_PARTS + EARLY + LAGS[-1]):
+            queue.tick(late)
         save_first = pltpu.make_async_copy(total, first_out, load_sem.at[0])
         save_gm = pltpu.make_async_copy(acts.at[:, pl.ds(width, width)], gm_out, load_sem.at[1])
         save_first.start()
@@ -1339,7 +1348,7 @@
         saves = [pltpu.make_async_copy(stage.at[BACK + n], tail_out.at[n], load_sem.at[n]) for n in range(2)]
         for save in saves:
             save.start()
-        for beat in range(16, 19):
+        for beat in range(16, 12 + LAGS[-1]):
             queue.tick(beat)
         queue.finish()
         for save in saves:

time: 369 us -> 368 us (level)
  no operation moved by 1% of the time
where the time goes in v1:
time: 368 us; the launch traced here: 361 us
  Pallas kernels  355 us (96%)
  local copies, waits for them, and re-layouts  5.73 us (2%)
    pallas_call x1, Pallas kernels, encode(): pl.pallas_call(encode_kernel, out_shape=[jax.ShapeDtypeStruct(own, BF16),...  146 us
    pallas_call x1, Pallas kernels, feed_backward(): pl.pallas_call(backward_kernel, grid=(4 + FF_PARTS,), out_shape=[jax.Shap...  85.8 us
    pallas_call x1, Pallas kernels, attend_back(): pl.pallas_call(attend_back_kernel, grid=(groups, rows, 2), out_shape=[jax...  63.8 us
    pallas_call x1, Pallas kernels, finish(): pl.pallas_call(finish_kernel, out_shape=[jax.ShapeDtypeStruct((32, width)...  30.3 us
    pallas_call x1, Pallas kernels, feed_forward(): pl.pallas_call(forward_kernel, grid=(FORWARD + tokens // 256,), out_shape...  22.8 us

profile of v1, /device:TPU:0, one launch (start us, length us, event | category | flops | bytes accessed | tf_op | source)
XLA Modules:
  0.0 361.3 jit_solution(323148853215906363)
XLA Ops:
  0.7 0.7 pad_dynamic-slice_fusion
  1.4 0.6 broadcast_in_dim.8.query_ids
  2.0 0.7 fusion
  2.6 1.3 copy.35.key_ids
  3.9 145.8 %gather_encode.1 = (bf16[2,512,1024]{2,1,0:T(8,128)(2,1)}, bf16[2,768,1024]{2,1,0:T(8,128)(2,1)}, bf16[2,768,1024]{2,1,0:T(8,128)(2,1)}, bf16[2,768,1024]{2,1,0:...) custom-call(bf16[2,512,1024]{2,1,0:T(8,128)(2,1)} %x_in.1, ...), custom_call_target="tpu_custom_call" | custom-call | tf_op jit(solution)/shard_map/gather_encode/pallas_call | solution.py:937
  149.7 22.8 %feed_forward.1 = (bf16[1024,1024]{1,0:T(8,128)(2,1)}, bf16[1024,1024]{1,0:T(8,128)(2,1)}, f32[1024,1024]{1,0:T(8,128)}, f32[8,1024]{1,0:T(8,128)}) custom-call(bf16[1024,4096]{1,0:T(8,128)(2,1)} %get-tuple-element.65.active.active_in, bf16[32,128,1024]{2,1,0:T(8,128)(2,1)} %bitcast.44, f32[1024,1024]{1,0:T(8,128)} %bitcast.46, bf16[1024,1024]{1,0:T(8,128)(2,1)} %bitcast.52, ...), custom_call_target="tpu_custom_call" | custom-call | tf_op jit(solution)/shard_map/feed_forward/pallas_call | solution.py:1042
  172.5 85.8 %feed_backward.1 = (f32[128,1024]{1,0:T(8,128)}, f32[32,2560]{1,0:T(8,128)}, bf16[5,2,2,4,2,32,512]{6,5,4,3,2,1,0:T(8,128)(2,1)}, f32[8,1,512]{2,1,0:T(1,128)}, ...) custom-call(bf16[1024,4096]{1,0:T(8,128)(2,1)} %get-tuple-element.65.active.active_in, ...), custom_call_target="tpu_custom_call" | custom-call | tf_op jit(solution)/shard_map/feed_backward/pallas_call | solution.py:1191
  258.3 63.8 %attend_back.1 = (bf16[2,512,1024]{2,1,0:T(8,128)(2,1)}, bf16[2,768,1024]{2,1,0:T(8,128)(2,1)}, bf16[2,768,1024]{2,1,0:T(8,128)(2,1)}, bf16[2,2,2,4,2,32,512]{6,...) custom-call(bf16[2,512,1024]{2,1,0:T(8,128)(2,1)} %get-tuple-element, ...), custom_call_target="tpu_custom_call" | custom-call | tf_op jit(solution)/shard_map/attend_back/pallas_call | solution.py:1367
  322.1 30.3 %sum_gradients.1 = (f32[32,1024]{1,0:T(8,128)}, f32[32,1024]{1,0:T(8,128)}, f32[32,1024]{1,0:T(8,128)}, f32[16,128]{1,0:T(8,128)}, f32[2,512,1024]{2,1,0:T(8,128)}, /*index=5*/bf16[2,256,1024]{2,1,0:T(8,128)(2,1)}) custom-call(bf16[2,2,2,4,2,32,512]{6,5,4,3,2,1,0:T(8,128)(2,1)} %get-tuple-element.86.tail_in, f32[8,1024]{1,0:T(8,128)} %get-tuple-element.87.sums0, ...), custom_call_target="tpu_custom_call" | custom-call | tf_op jit(solution)/shard_map/sum_gradients/pallas_call | solution.py:1536
  352.4 6.2 %deliver.1 = (f32[2,512,1024]{2,1,0:T(8,128)}, f32[32,1024]{1,0:T(8,128)}, f32[32,1024]{1,0:T(8,128)}, f32[32,1024]{1,0:T(8,128)}, f32[32,1024]{1,0:T(8,128)}, /...) custom-call(f32[2,512,1024]{2,1,0:T(8,128)} %get-tuple-element.96.gh, ...), custom_call_target="tpu_custom_call" | custom-call | tf_op jit(solution)/shard_map/deliver/pallas_call | solution.py:1586
  358.6 1.2 slice_bitcast_fusion.3
  359.8 0.7 slice.34
  360.5 0.1 reshape.135
  360.6 0.5 slice_bitcast_fusion
